TPU v7x, 256 devices: a whole 4x4x8 slice. The times are simulated.
256 devices in a mesh: ctx: 8 (over x, core), exp: 32 (over y, z).
Axes of the slice: x: 4, y: 4, z: 8, core: 2. Of those that a mesh axis runs over, the one named last changes fastest.
Arguments:
- tokens_in: bfloat16 [1024, 6144], P('ctx'), may hold values from -6 to 6
- queries: bfloat16 [1024, 8192], P('ctx', 'exp'), may hold values from -6 to 6
- keys: bfloat16 [1024, 8192], P('ctx', 'exp'), may hold values from -6 to 6
- values: bfloat16 [1024, 8192], P('ctx', 'exp'), may hold values from -6 to 6
- log_decay: float32 [64, 1024], P('exp', 'ctx'), may hold values from -1.3 to 0
- incoming_state: float32 [64, 128, 128], P('exp'), may hold values from -12 to 12
- attn_gain: float32 [8192], P('exp'), may hold values from 0.1 to 1.9
- w_out: bfloat16 [8192, 6144], P('exp'), may hold values from -0.0625 to 0.0625
- ffn_gain: float32 [6144], replicated, may hold values from 0.1 to 1.9
- router: bfloat16 [6144, 4], replicated, may hold values from -0.078125 to 0.078125
- expert_ids: int32 [1024, 2], P('ctx'), may hold values from 0 to 3, all different within a row; in each aligned block of 128 rows (0 to 127, 128 to 255, ...) at most 80 rows name the same one
- w_in: bfloat16 [2, 36864, 6144], P(None, ('exp', 'ctx')), may hold values from -0.078125 to 0.078125
- w_down: bfloat16 [36864, 6144], P(('exp', 'ctx')), may hold values from -0.0625 to 0.0625
Outputs:
- mixed: bfloat16 [1024, 6144], P('ctx', 'exp')
Inputs may be any that keep to these rules, and one draw needn't show every extreme that they name: `expert_ids`: A token's two experts differ. Among the 128 tokens of one index of ctx no expert is named by more than 80 tokens, a bound that some block reaches of them.
All inputs are finite; a program needn't handle non-finite values.
Results may differ from a plain program's by a relative error of at most 0.027.
Values may be sent and summed in bfloat16 or wider, within the bound.
A program may use at most 128 MiB of HBM per device.

v0:
```python
import jax
import jax.numpy as jnp
from jax import lax
from jax.sharding import PartitionSpec as P

FF = 9216
CAP = 80
HIGHEST = lax.Precision.HIGHEST
epsilon = 1e-06


def shifted(value, axis, steps):
    count = lax.axis_size(axis)
    initial, last = (max(0, -steps), min(count, count - steps))
    return lax.ppermute(value, axis, [(source, source + steps) for source in range(initial, last)])


def rms_scale(values_f32, gain):
    mean_square = jnp.mean(values_f32 * values_f32, axis=-1, keepdims=True)
    return values_f32 * lax.rsqrt(mean_square + epsilon) * gain


def local(
    tokens_in,
    queries,
    keys,
    values,
    log_decay,
    incoming_state,
    attn_gain,
    w_out,
    ffn_gain,
    router,
    expert_ids,
    w_in,
    w_down,
):
    row_count = queries.shape[0]
    head_count = incoming_state.shape[0]
    head_size = incoming_state.shape[1]
    scale = head_size ** (-0.5)
    q_heads = queries.reshape(row_count, head_count, head_size)
    k_heads = keys.reshape(row_count, head_count, head_size)
    v_float = values.reshape(row_count, head_count, head_size).astype(jnp.float32)
    cumulative = jnp.cumsum(log_decay, axis=1)
    decay_total = jnp.exp(cumulative[:, -1])
    tail = jnp.exp(cumulative[:, -1:] - cumulative)
    key_scaled = k_heads.astype(jnp.float32) * tail.T[:, :, None]
    local_state = jnp.einsum("thd,the->hde", key_scaled, v_float, precision=HIGHEST)
    leading = lax.axis_index("ctx") == 0
    state_in = jnp.where(leading, incoming_state, jnp.zeros_like(incoming_state))
    for hop_index in range(lax.axis_size("ctx") - 1):
        outgoing = decay_total[:, None, None] * state_in + local_state
        arrived = shifted(outgoing.astype(jnp.bfloat16), "ctx", 1).astype(outgoing.dtype)
        state_in = jnp.where(leading, incoming_state, arrived)
    positions = lax.iota(jnp.int32, row_count)
    lower = (positions[:, None] >= positions[None, :])[None, :, :]
    gap = jnp.where(lower, cumulative[:, :, None] - cumulative[:, None, :], 0.0)
    weight = jnp.where(lower, jnp.exp(gap), 0.0)
    scores = (
        jnp.einsum("thd,shd->hts", q_heads, k_heads, preferred_element_type=jnp.float32)
        * scale
        * weight
    )
    query_scaled = q_heads.astype(jnp.float32) * (scale * jnp.exp(cumulative)).T[:, :, None]
    attended = jnp.einsum("hts,she->the", scores, v_float, precision=HIGHEST) + jnp.einsum(
        "thd,hde->the", query_scaled, state_in, precision=HIGHEST
    )
    attn_heads = (
        rms_scale(attended, attn_gain.reshape(head_count, head_size))
        .astype(jnp.bfloat16)
        .reshape(row_count, head_count * head_size)
    )
    width = tokens_in.shape[1]
    exp_count = lax.axis_size("exp")
    attn_full = lax.psum(
        jnp.dot(attn_heads, w_out, preferred_element_type=jnp.float32).astype(jnp.bfloat16), "exp"
    ).astype(jnp.float32)
    mid_full = tokens_in.astype(jnp.float32) + attn_full
    normed = rms_scale(mid_full, ffn_gain).astype(jnp.bfloat16)
    expert_count = router.shape[1]
    logits = jnp.dot(normed, router, preferred_element_type=jnp.float32)
    picked = expert_ids[:, :, None] == lax.iota(jnp.int32, expert_count)[None, None, :]
    chosen = jnp.sum(jnp.where(picked, logits[:, None, :], 0.0), axis=2)
    sigmoid_gate = jax.nn.sigmoid(chosen)
    gates = sigmoid_gate / jnp.sum(sigmoid_gate, axis=1, keepdims=True)
    slice_units = w_in.shape[1]
    block_index = lax.axis_index("exp") * lax.axis_size("ctx") + lax.axis_index("ctx")
    owned = block_index * slice_units // FF
    paired = w_in.reshape(2 * slice_units, width)
    flat_routes = expert_ids.reshape(row_count * 2)
    one_hot = (flat_routes[:, None] == lax.iota(jnp.int32, expert_count)[None, :]).astype(jnp.int32)
    earlier_count = jnp.cumsum(one_hot, axis=0) - one_hot
    slot_of = jnp.sum(earlier_count * one_hot, axis=1).reshape(row_count, 2)
    capacity = CAP
    in_slot = (expert_ids == owned)[:, :, None] & (
        slot_of[:, :, None] == lax.iota(jnp.int32, capacity)[None, None, :]
    )
    placement = jnp.any(in_slot, axis=1).T.astype(jnp.bfloat16)
    slot_buffer = jnp.dot(placement, normed, preferred_element_type=jnp.float32).astype(
        jnp.bfloat16
    )
    combine = jnp.sum(jnp.where(in_slot, gates[:, :, None], 0.0), axis=1)
    projected = lax.dot_general(
        lax.all_gather(slot_buffer, "ctx", axis=0, tiled=True),
        paired,
        (((1,), (1,)), ((), ())),
        preferred_element_type=jnp.float32,
    )
    hidden = (jax.nn.silu(projected[:, :slice_units]) * projected[:, slice_units:]).astype(
        jnp.bfloat16
    )
    partials = jnp.dot(hidden, w_down, preferred_element_type=jnp.float32).astype(jnp.bfloat16)
    summed = lax.psum_scatter(
        partials.astype(jnp.float32).astype(jnp.bfloat16), "ctx", scatter_dimension=0, tiled=True
    ).astype(jnp.float32)
    contrib = jnp.dot(combine, summed, precision=HIGHEST)
    column_count = width // exp_count
    column_start = lax.axis_index("exp") * column_count
    residual = lax.dynamic_slice_in_dim(mid_full, column_start, column_count, 1)
    total = lax.psum_scatter(
        contrib.astype(jnp.bfloat16), "exp", scatter_dimension=1, tiled=True
    ).astype(jnp.float32)
    return (total + residual).astype(jnp.bfloat16)


def solution(mesh):
    return jax.shard_map(
        local,
        mesh=mesh,
        in_specs=(
            P("ctx", None),
            P("ctx", "exp"),
            P("ctx", "exp"),
            P("ctx", "exp"),
            P("exp", "ctx"),
            P("exp", None, None),
            P("exp"),
            P("exp", None),
            P(),
            P(),
            P("ctx", None),
            P(None, ("exp", "ctx"), None),
            P(("exp", "ctx"), None),
        ),
        out_specs=P("ctx", "exp"),
        check_vma=False,
    )
```

profile of v0, /device:TPU:2, one launch (start us, length us, event | category | flops | bytes accessed | tf_op | source)
XLA Modules:
  0.0 555.5 jit_solution(10375486550913919019)
XLA Ops:
  6.5 1.1 reduce_window_sum.28
  7.9 1.6 copy.73
  9.5 1.2 add_convert_fusion.7
  10.8 1.9 collective-permute-start
  12.7 3.7 collective-permute-done
  16.4 1.9 collective-permute-start.1
  18.4 3.7 collective-permute-done.1
  22.1 1.9 collective-permute-start.2
  24.0 3.7 collective-permute-done.2
  27.8 1.9 collective-permute-start.3
  29.7 3.7 collective-permute-done.3
  33.5 1.9 collective-permute-start.4
  35.4 3.6 collective-permute-done.4
  39.1 1.9 collective-permute-start.5
  42.1 2.6 collective-permute-done.5
  44.8 1.9 collective-permute-start.6
  47.9 2.5 collective-permute-done.6
  51.0 1.8 convolution_convert_fusion.2
  55.6 1.2 reduce-window.6
  61.9 145.4 %all-reduce.2.cloned.1.call-done = bf16[128,6144]{1,0:T(8,128)(2,1)} async-done(((bf16[128,6144]{1,0:T(8,128)(2,1)}), bf16[128,6144]{1,0:T(8,128)(2,1)}) %all-reduce.2.cloned.1.call-update) | async-done | bytes 1572880 | tf_op jit(solution)/shard_map/psum | solution.py:76
  207.3 4.3 multiply_reduce_fusion
  212.2 1.9 convolution_convert_fusion.3
  214.1 46.6 %all-gather.2.cloned.1.call-done = bf16[640,6144]{1,0:T(8,128)(2,1)} async-done(((bf16[80,6144]{1,0:T(8,128)(2,1)}), bf16[640,6144]{1,0:T(8,128)(2,1)}) %all-gather.2.cloned.1.call-update) | async-done | bytes 7864336 | tf_op jit(solution)/shard_map/all_gather | solution.py:105
  260.7 5.4 fusion.31
  266.1 5.4 convolution_convert_fusion
  271.6 2.6 fusion.30
  274.9 47.8 %reduce-scatter.5.cloned.1.call-done = bf16[80,6144]{1,0:T(8,128)(2,1)} async-done(((bf16[640,6144]{1,0:T(8,128)(2,1)}), bf16[80,6144]{1,0:T(8,128)(2,1)}) %reduce-scatter.5.cloned.1.call-update) | async-done | bytes 983056 | tf_op jit(solution)/shard_map/reduce_scatter | solution.py:114
  322.7 4.1 fusion
  326.9 217.3 %reduce-scatter.7.cloned.1.call-done = bf16[192,128]{1,0:T(8,128)(2,1)} async-done(((bf16[6144,128]{1,0:T(8,128)(2,1)}), bf16[192,128]{1,0:T(8,128)(2,1)}) %reduce-scatter.7.cloned.1.call-update) | async-done | bytes 49168
  544.3 1.5 copy.72
  545.8 1.7 add_convert_fusion
  547.4 1.6 copy.69
  (71 shorter events, 12.7 us)
Async XLA Ops:
  6.5 254.1 %copy-start = (bf16[2,144,6144]{2,1,0:T(8,128)(2,1)S(1)}, bf16[2,144,6144]{2,1,0:T(8,128)(2,1)}, u32[]{:S(2)}) copy-start(bf16[2,144,6144]{2,1,0:T(8,128)(2,1)} %param.24) | copy-start | bytes 10616836
  6.5 200.8 %all-reduce.2.cloned.1.call-start = ((), (), s32[]{:S(2)}) async-start(), calls=%async_computation.2 | async-start | bytes 3145728 | tf_op jit(solution)/shard_map/psum | solution.py:76
  9.5 40.9 %copy-start.1 = (f32[2,128,128]{2,1,0:T(8,128)S(1)}, f32[2,128,128]{2,1,0:T(8,128)}, u32[]{:S(2)}) copy-start(f32[2,128,128]{2,1,0:T(8,128)} %param.18) | copy-start | bytes 393220
  9.5 40.9 %copy-start.6 = (bf16[128,256]{1,0:T(8,128)(2,1)S(1)}, bf16[128,256]{1,0:T(8,128)(2,1)}, u32[]{:S(2)}) copy-start(bf16[128,256]{1,0:T(8,128)(2,1)} %param.14) | copy-start | bytes 196612
  9.5 41.4 %copy-start.12 = (f32[256]{0:T(256)S(1)}, f32[256]{0:T(256)}, u32[]{:S(2)}) copy-start(f32[256]{0:T(256)} %param.19) | copy-start | bytes 3076
  9.5 41.5 %copy-start.4 = (bf16[256,6144]{1,0:T(8,128)(2,1)S(1)}, bf16[256,6144]{1,0:T(8,128)(2,1)}, u32[]{:S(2)}) copy-start(bf16[256,6144]{1,0:T(8,128)(2,1)} %param.20) | copy-start | bytes 9437188
  10.8 5.6 %collective-permute-start = (bf16[2,128,128]{2,1,0:T(8,128)(2,1)S(1)}, bf16[2,128,128]{2,1,0:T(8,128)(2,1)S(1)}, u32[]{:S(2)}, u32[]{:S(2)}) collective-permute-start(bf16[2,128,128]{2,1,0:T(8,128)(2,1)S(1)} %get-tuple-element.9), channel_id=1, source_target_pairs={{0,32},{32,64},{64,96},{96,128},{128,160},{160,192},{192,224},{1,3... | collective-permute-start | bytes 196616 | tf_op jit(solution)/shard_map/ppermute | solution.py:15
  16.4 5.6 %collective-permute-start.1 = (bf16[2,128,128]{2,1,0:T(8,128)(2,1)S(1)}, bf16[2,128,128]{2,1,0:T(8,128)(2,1)S(1)}, u32[]{:S(2)}, u32[]{:S(2)}) collective-permute-start(bf16[2,128,128]{2,1,0:T(8,128)(2,1)S(1)} %add_convert_fusion.6), channel_id=1, source_target_pairs={{0,32},{32,64},{64,96},{96,128},{128,160},{160,192},{192,224},{1,3... | collective-permute-start | bytes 196616 | tf_op jit(solution)/shard_map/ppermute | solution.py:15
  22.1 5.6 %collective-permute-start.2 = (bf16[2,128,128]{2,1,0:T(8,128)(2,1)S(1)}, bf16[2,128,128]{2,1,0:T(8,128)(2,1)S(1)}, u32[]{:S(2)}, u32[]{:S(2)}) collective-permute-start(bf16[2,128,128]{2,1,0:T(8,128)(2,1)S(1)} %add_convert_fusion.5), channel_id=1, source_target_pairs={{0,32},{32,64},{64,96},{96,128},{128,160},{160,192},{192,224},{1,3... | collective-permute-start | bytes 196616 | tf_op jit(solution)/shard_map/ppermute | solution.py:15
  27.8 5.6 %collective-permute-start.3 = (bf16[2,128,128]{2,1,0:T(8,128)(2,1)S(1)}, bf16[2,128,128]{2,1,0:T(8,128)(2,1)S(1)}, u32[]{:S(2)}, u32[]{:S(2)}) collective-permute-start(bf16[2,128,128]{2,1,0:T(8,128)(2,1)S(1)} %add_convert_fusion.4), channel_id=1, source_target_pairs={{0,32},{32,64},{64,96},{96,128},{128,160},{160,192},{192,224},{1,3... | collective-permute-start | bytes 196616 | tf_op jit(solution)/shard_map/ppermute | solution.py:15
  33.5 5.6 %collective-permute-start.4 = (bf16[2,128,128]{2,1,0:T(8,128)(2,1)S(1)}, bf16[2,128,128]{2,1,0:T(8,128)(2,1)S(1)}, u32[]{:S(2)}, u32[]{:S(2)}) collective-permute-start(bf16[2,128,128]{2,1,0:T(8,128)(2,1)S(1)} %add_convert_fusion.3), channel_id=1, source_target_pairs={{0,32},{32,64},{64,96},{96,128},{128,160},{160,192},{192,224},{1,3... | collective-permute-start | bytes 196616 | tf_op jit(solution)/shard_map/ppermute | solution.py:15
  39.1 5.6 %collective-permute-start.5 = (bf16[2,128,128]{2,1,0:T(8,128)(2,1)S(1)}, bf16[2,128,128]{2,1,0:T(8,128)(2,1)S(1)}, u32[]{:S(2)}, u32[]{:S(2)}) collective-permute-start(bf16[2,128,128]{2,1,0:T(8,128)(2,1)S(1)} %add_convert_fusion.2), channel_id=1, source_target_pairs={{0,32},{32,64},{64,96},{96,128},{128,160},{160,192},{192,224},{1,3... | collective-permute-start | bytes 196616 | tf_op jit(solution)/shard_map/ppermute | solution.py:15
  44.8 5.6 %collective-permute-start.6 = (bf16[2,128,128]{2,1,0:T(8,128)(2,1)S(1)}, bf16[2,128,128]{2,1,0:T(8,128)(2,1)S(1)}, u32[]{:S(2)}, u32[]{:S(2)}) collective-permute-start(bf16[2,128,128]{2,1,0:T(8,128)(2,1)S(1)} %add_convert_fusion.1), channel_id=1, source_target_pairs={{0,32},{32,64},{64,96},{96,128},{128,160},{160,192},{192,224},{1,3... | collective-permute-start | bytes 196616 | tf_op jit(solution)/shard_map/ppermute | solution.py:15
  51.0 1.9 copy-start.8
  52.8 207.9 %all-gather.2.cloned.1.call-start = ((), (), s32[]{:S(2)}) async-start(), calls=%async_computation.3 | async-start | bytes 8847360 | tf_op jit(solution)/shard_map/all_gather | solution.py:105
  61.4 0.5 copy-start.10
  207.3 4.8 copy-start.2
  207.3 4.8 copy-start.3
  207.3 4.8 copy-start.7
  211.6 0.5 copy-start.13
  214.1 108.7 %reduce-scatter.5.cloned.1.call-start = ((), (), s32[]{:S(2)}) async-start(), calls=%async_computation.4 | async-start | bytes 8847360 | tf_op jit(solution)/shard_map/reduce_scatter | solution.py:114
  260.7 5.4 copy-start.5
  271.5 2.7 copy-start.9
  271.5 2.7 copy-start.11
  271.5 272.7 %reduce-scatter.7.cloned.1.call-start = ((), (), s32[]{:S(2)}) async-start(), calls=%async_computation.5 | async-start | bytes 1622016
Sparse Core Ops, SparseCore 0:
  52.9 154.3 all-reduce.1
  214.2 46.4 all-gather.1
  271.6 51.0 reduce-scatter.4
  327.0 217.1 reduce-scatter.6
where the time goes:
time: 556 us
  waiting for transfers between devices  481 us (87%)
  matrix products  25 us (4%)
  starting transfers between devices  13.6 us (2%)
  between operations  13.4 us (2%)
  local copies, waits for them, and re-layouts  12.3 us (2%)
  other arithmetic  10.6 us (2%)
    unnamed x5, waiting for transfers between devices  217 us
    psum x1, waiting for transfers between devices, local(): lax.psum(jnp.dot(attn_heads, w_out, preferred_element_type=jnp.float32).a...  145 us
    reduce_scatter x1, waiting for transfers between devices, local(): lax.psum_scatter(partials.astype(jnp.float32).astype(jnp.bfloat16), 'ctx'...  47.8 us
    all_gather x1, waiting for transfers between devices, local(): lax.all_gather(slot_buffer, 'ctx', axis=0, tiled=True)  46.6 us
    ppermute x7, waiting for transfers between devices, shifted(): lax.ppermute(value, axis, [(source, source + steps) for source in range(i...  23.4 us
    ppermute x7, starting transfers between devices, shifted(): lax.ppermute(value, axis, [(source, source + steps) for source in range(i...  13.4 us
  transfers between devices with their start and end apart: 11, of which 11 were waited for; matrix products, arithmetic and copies ran while one was open for 3% of the time, Pallas kernels for 0%

commit v1 on v0

--- a/solution.py
+++ b/solution.py
@@ -73,8 +73,12 @@
     )
     width = tokens_in.shape[1]
     exp_count = lax.axis_size("exp")
-    attn_full = lax.psum(
-        jnp.dot(attn_heads, w_out, preferred_element_type=jnp.float32).astype(jnp.bfloat16), "exp"
+    attn_full = jnp.sum(
+        lax.all_gather(
+            jnp.dot(attn_heads, w_out, preferred_element_type=jnp.float32).astype(jnp.bfloat16),
+            "exp",
+        ),
+        axis=0,
     ).astype(jnp.float32)
     mid_full = tokens_in.astype(jnp.float32) + attn_full
     normed = rms_scale(mid_full, ffn_gain).astype(jnp.bfloat16)

time: 556 us -> 755 us (1.36)
  waiting for transfers between devices: 481 us -> 658 us
  other arithmetic: 10.6 us -> 28.2 us
    all_gather x0 -> x1, waiting for transfers between devices: none -> 324 us  [local(): lax.all_gather(jnp.dot(attn_heads, w_out, preferred_element_type=jnp.floa...]
    reduce_scatter x0 -> x1, waiting for transfers between devices: none -> 217 us  [local(): lax.psum_scatter(contrib.astype(jnp.bfloat16), 'exp', scatter_dimension=1...]
    unnamed x5 -> x4, waiting for transfers between devices: 217 us -> 0.07 us
    psum x1 -> x0, waiting for transfers between devices: 145 us -> none  [local(): lax.psum(jnp.dot(attn_heads, w_out, preferred_element_type=jnp.float32).a...]
    reduce_sum x0 -> x1, other arithmetic: none -> 17.6 us  [local(): jnp.sum(lax.all_gather(jnp.dot(attn_heads, w_out, preferred_element_type=...]
  transfers between devices with their start and end apart: 11 -> 11, of which waited for: 11 -> 11; matrix products, arithmetic and copies ran while one was open for 3% -> 2% of each run, Pallas kernels for 0% -> 0%
where the time goes in v1:
time: 755 us; the launch traced here: 754 us
  waiting for transfers between devices  658 us (87%)
  other arithmetic  28.2 us (4%)
  matrix products  25.6 us (3%)
  local copies, waits for them, and re-layouts  14.4 us (2%)
  starting transfers between devices  13.8 us (2%)
  between operations  13.4 us (2%)
    all_gather x1, waiting for transfers between devices, local(): lax.all_gather(jnp.dot(attn_heads, w_out, preferred_element_type=jnp.floa...  324 us
    reduce_scatter x1, waiting for transfers between devices, local(): lax.psum_scatter(contrib.astype(jnp.bfloat16), 'exp', scatter_dimension=1...  217 us
    reduce_scatter x1, waiting for transfers between devices, local(): lax.psum_scatter(partials.astype(jnp.float32).astype(jnp.bfloat16), 'ctx'...  47.4 us
    all_gather x1, waiting for transfers between devices, local(): lax.all_gather(slot_buffer, 'ctx', axis=0, tiled=True)  46.4 us
    ppermute x7, waiting for transfers between devices, shifted(): lax.ppermute(value, axis, [(source, source + steps) for source in range(i...  23.4 us
    reduce_sum x1, other arithmetic, local(): jnp.sum(lax.all_gather(jnp.dot(attn_heads, w_out, preferred_element_type=...  17.6 us
  transfers between devices with their start and end apart: 11, of which 11 were waited for; matrix products, arithmetic and copies ran while one was open for 2% of the time, Pallas kernels for 0%

profile of v1, /device:TPU:2, one launch (start us, length us, event | category | flops | bytes accessed | tf_op | source)
XLA Modules:
  0.0 753.8 jit_solution(5255698724520275399)
XLA Ops:
  7.9 1.6 copy.69
  9.5 1.2 add_convert_fusion.6
  10.8 1.9 collective-permute-start
  12.7 3.7 collective-permute-done
  16.4 1.9 collective-permute-start.1
  18.4 3.7 collective-permute-done.1
  22.1 1.9 collective-permute-start.2
  24.0 3.7 collective-permute-done.2
  27.8 1.9 collective-permute-start.3
  29.7 3.7 collective-permute-done.3
  33.5 1.9 collective-permute-start.4
  35.4 3.6 collective-permute-done.4
  39.1 1.9 collective-permute-start.5
  42.1 2.6 collective-permute-done.5
  44.8 1.9 collective-permute-start.6
  47.9 2.5 collective-permute-done.6
  51.0 1.7 convolution_convert_fusion.2
  55.5 2.6 copy.59
  58.2 1.2 reduce-window.6
  64.5 323.8 %all-gather.6.cloned.1.call-done = bf16[4096,6144]{1,0:T(8,128)(2,1)} async-done(((bf16[128,6144]{1,0:T(8,128)(2,1)}), bf16[4096,6144]{1,0:T(8,128)(2,1)}) %all-gather.6.cloned.1.call-update) | async-done | bytes 50331664 | tf_op jit(solution)/shard_map/all_gather | solution.py:77
  388.2 17.6 %reduce_sum.68 = bf16[128,6144]{1,0:T(8,128)(2,1)} reduce(bf16[32,128,6144]{2,1,0:T(8,128)(2,1)} %bitcast.76, bf16[]{:T(256)} %constant.54.clone.1), dimensions={0}, to_apply=%region_5.6 | reduce | flops 24379392 | bytes 51904512 | tf_op jit(solution)/shard_map/reduce_sum | solution.py:76
  405.8 2.6 copy.67
  408.4 4.5 multiply_reduce_fusion
  413.4 2.2 convolution_convert_fusion.3
  415.7 46.4 %all-gather.4.cloned.1.call-done = bf16[640,6144]{1,0:T(8,128)(2,1)} async-done(((bf16[80,6144]{1,0:T(8,128)(2,1)}), bf16[640,6144]{1,0:T(8,128)(2,1)}) %all-gather.4.cloned.1.call-update) | async-done | bytes 7864336 | tf_op jit(solution)/shard_map/all_gather | solution.py:109
  462.1 5.4 fusion.30
  467.6 5.4 convolution_convert_fusion
  473.2 2.9 fusion.29
  476.8 47.4 %reduce-scatter.3.cloned.1.call-done = bf16[80,6144]{1,0:T(8,128)(2,1)} async-done(((bf16[640,6144]{1,0:T(8,128)(2,1)}), bf16[80,6144]{1,0:T(8,128)(2,1)}) %reduce-scatter.3.cloned.1.call-update) | async-done | bytes 983056 | tf_op jit(solution)/shard_map/reduce_scatter | solution.py:118
  524.2 4.1 convolution_convert_fusion.1
  528.3 217.4 %reduce-scatter.5.cloned.1.call-done = bf16[128,192]{0,1:T(8,128)(2,1)} async-done(((bf16[128,6144]{0,1:T(8,128)(2,1)}), bf16[128,192]{0,1:T(8,128)(2,1)}) %reduce-scatter.5.cloned.1.call-update) | async-done | bytes 49168 | tf_op jit(solution)/shard_map/reduce_scatter | solution.py:125
  745.7 1.5 add_convert_fusion.7
  (72 shorter events, 14.0 us)
Async XLA Ops:
  6.5 455.6 %copy-start = (bf16[2,144,6144]{2,1,0:T(8,128)(2,1)S(1)}, bf16[2,144,6144]{2,1,0:T(8,128)(2,1)}, u32[]{:S(2)}) copy-start(bf16[2,144,6144]{2,1,0:T(8,128)(2,1)} %param.24) | copy-start | bytes 10616836
  6.5 381.7 %all-gather.6.cloned.1.call-start = ((), (), s32[]{:S(2)}) async-start(), calls=%async_computation.5 | async-start | bytes 51904512 | tf_op jit(solution)/shard_map/all_gather | solution.py:77
  9.5 40.9 %copy-start.3 = (f32[2,128,128]{2,1,0:T(8,128)S(1)}, f32[2,128,128]{2,1,0:T(8,128)}, u32[]{:S(2)}) copy-start(f32[2,128,128]{2,1,0:T(8,128)} %param.18) | copy-start | bytes 393220
  9.5 40.9 %copy-start.6 = (bf16[128,256]{1,0:T(8,128)(2,1)S(1)}, bf16[128,256]{1,0:T(8,128)(2,1)}, u32[]{:S(2)}) copy-start(bf16[128,256]{1,0:T(8,128)(2,1)} %param.14) | copy-start | bytes 196612
  9.5 41.4 %copy-start.12 = (f32[256]{0:T(256)S(1)}, f32[256]{0:T(256)}, u32[]{:S(2)}) copy-start(f32[256]{0:T(256)} %param.19) | copy-start | bytes 3076
  9.5 41.5 %copy-start.4 = (bf16[256,6144]{1,0:T(8,128)(2,1)S(1)}, bf16[256,6144]{1,0:T(8,128)(2,1)}, u32[]{:S(2)}) copy-start(bf16[256,6144]{1,0:T(8,128)(2,1)} %param.20) | copy-start | bytes 9437188
  10.8 5.6 collective-permute-start
  16.4 5.6 collective-permute-start.1
  22.1 5.6 collective-permute-start.2
  27.8 5.6 collective-permute-start.3
  33.5 5.6 collective-permute-start.4
  39.1 5.6 collective-permute-start.5
  44.8 5.6 collective-permute-start.6
  51.0 1.9 copy-start.8
  52.8 409.3 %all-gather.4.cloned.1.call-start = ((), (), s32[]{:S(2)}) async-start(), calls=%async_computation.2 | async-start | bytes 8847360 | tf_op jit(solution)/shard_map/all_gather | solution.py:109
  63.9 0.5 copy-start.10
  408.4 5.1 copy-start.1
  408.4 5.1 copy-start.2
  408.4 5.1 copy-start.7
  412.9 0.5 copy-start.13
  415.7 108.5 %reduce-scatter.3.cloned.1.call-start = ((), (), s32[]{:S(2)}) async-start(), calls=%async_computation.3 | async-start | bytes 8847360 | tf_op jit(solution)/shard_map/reduce_scatter | solution.py:118
  462.1 5.4 copy-start.5
  472.9 3.2 copy-start.9
  472.9 3.2 copy-start.11
  473.0 272.8 %reduce-scatter.5.cloned.1.call-start = ((), (), s32[]{:S(2)}) async-start(), calls=%async_computation.4 | async-start | bytes 1622016 | tf_op jit(solution)/shard_map/reduce_scatter | solution.py:125
Sparse Core Ops, SparseCore 0:
  52.9 335.2 all-gather.5
  415.8 46.2 all-gather.3
  473.1 51.0 reduce-scatter.2
  528.5 217.2 reduce-scatter.4
